TPU v7x, 768 devices: a whole 4x8x12 slice. The times are simulated.
768 devices in a mesh: pair: 64 (over y, x, core), panel: 12 (over z).
Axes of the slice: x: 4, y: 8, z: 12, core: 2. Of those that a mesh axis runs over, the one named last changes fastest.
Arguments:
- amps: bfloat16 [32768, 6144], P('pair', 'panel'), may hold values from -6 to 6
- pair_energy: float32 [32768], P('pair'), may hold values from -2 to -0.5
- virt_energy: float32 [6144], P('panel'), may hold values from 0.5 to 4
- ladder_rows: int32 [64, 48, 16], P('pair', 'panel'), may hold values from 0 to 47, as said below
- ladder_count: int32 [64, 48], P('pair', 'panel'), may hold values from 1 to 16, as said below
- ladder_tiles: bfloat16 [64, 768, 128, 128], P('pair', 'panel'), may hold values from -0.1875 to 0.1875
- cycle_owner: int32 [49152, 1], P(('pair', 'panel')), may hold values from 0 to 63; in each aligned block of 64 rows (0 to 63, 64 to 127, ...) at most 2 rows name the same one
- cycle_slot: int32 [49152, 1], P(('pair', 'panel')), may hold values from 0 to 15
- cycle_tiles: bfloat16 [64, 192, 128, 128], P('pair', 'panel'), may hold values from -0.5 to 0.5
Outputs:
- residual: float32 [32768, 6144], P('pair', 'panel')
Inputs may be any that keep to these rules, and one draw needn't show every extreme that they name: `ladder_rows`: each list names 16 different tiles. Only the first ladder_count entries of a list are live; in every draw some list is full. `cycle_owner`: in the 64 rows of one device no pair index is named more than 2 times, and some index reaches it.
All inputs are finite; a program needn't handle non-finite values.
Results may differ from a plain program's by a relative error of at most 0.00075.
Values may be sent and summed in bfloat16 or wider, within the bound.
A program may use at most 64 MiB of HBM per device.

v0:
```python
import jax
import jax.numpy as jnp
from jax import lax
from jax.sharding import PartitionSpec as P

TB = 128
LMAX = 16
RR = 32


def on_device(
    amps,
    pair_energy,
    virt_energy,
    ladder_rows,
    ladder_count,
    ladder_tiles,
    cycle_owner,
    cycle_slot,
    cycle_tiles,
):
    slab_rows = amps.shape[0]
    col_tiles = amps.shape[1] // TB
    all_tiles = col_tiles * lax.axis_size("panel")
    lists = ladder_rows[0]
    counts = ladder_count[0]
    live_mask = lax.broadcasted_iota(jnp.int32, (col_tiles, LMAX), 1) < counts[:, None]
    listed = ladder_tiles[0].reshape(col_tiles, LMAX, TB, TB)
    gathered = lax.all_gather(amps, "panel", axis=1, tiled=True)
    picked = jnp.take(gathered.reshape(slab_rows, all_tiles, TB), lists.reshape(-1), axis=1)
    masked = listed * live_mask.astype(jnp.bfloat16)[:, :, None, None]
    ladder = jnp.einsum(
        "rkc,kcd->rkd",
        picked.reshape(slab_rows, col_tiles, LMAX * TB),
        masked.reshape(col_tiles, LMAX * TB, TB),
        preferred_element_type=jnp.float32,
    )
    ladder = ladder.reshape(slab_rows, col_tiles * TB)
    tile_total = cycle_owner.shape[0]
    pair_count = lax.axis_size("pair")
    capacity = max(2, 2 * tile_total // pair_count)
    target = cycle_owner[:, 0]
    which_mat = cycle_slot[:, 0]
    target_hot = (
        target[:, None] == lax.broadcasted_iota(jnp.int32, (tile_total, pair_count), 1)
    ).astype(jnp.int32)
    earlier = jnp.cumsum(target_hot, axis=0) - target_hot
    rank_within = jnp.sum(earlier * target_hot, axis=1)
    position = target * capacity + rank_within
    amp_tiles = (
        amps.reshape(slab_rows // RR, RR, col_tiles, TB)
        .transpose(0, 2, 1, 3)
        .reshape(tile_total, RR, TB)
    )
    send_tiles = (
        jnp.zeros((pair_count * capacity, RR, TB), jnp.bfloat16).at[position].set(amp_tiles)
    )
    send_tiles = send_tiles.reshape(pair_count, capacity, RR, TB)
    send_index = (
        jnp.zeros((pair_count * capacity,), jnp.bfloat16)
        .at[position]
        .set(which_mat.astype(jnp.bfloat16))
    )
    send_index = send_index.reshape(pair_count, capacity)
    own_mats = cycle_tiles[0]
    got_tiles = lax.all_to_all(send_tiles, "pair", split_axis=0, concat_axis=0, tiled=True)
    got_index = lax.all_to_all(send_index, "pair", split_axis=0, concat_axis=0, tiled=True)
    mat_index = got_index.reshape(-1).astype(jnp.int32)
    mats = jnp.take(own_mats, mat_index, axis=0)
    flat_tiles = got_tiles.reshape(-1, RR, TB)
    product = jnp.einsum(
        "src,scd->srd", flat_tiles, mats, preferred_element_type=jnp.float32
    ).astype(jnp.bfloat16)
    returned = lax.all_to_all(
        product.reshape(got_tiles.shape), "pair", split_axis=0, concat_axis=0, tiled=True
    )
    cycle = jnp.take(returned.reshape(pair_count * capacity, RR, TB), position, axis=0)
    cycle = (
        cycle.reshape(slab_rows // RR, col_tiles, RR, TB)
        .transpose(0, 2, 1, 3)
        .reshape(slab_rows, col_tiles * TB)
    )
    energies = virt_energy[None, :] - pair_energy[:, None]
    return energies * amps.astype(jnp.float32) + ladder + cycle.astype(jnp.float32)


def solution(mesh):
    in_specs = (
        P("pair", "panel"),
        P("pair"),
        P("panel"),
        P("pair", "panel", None),
        P("pair", "panel"),
        P("pair", "panel", None, None),
        P(("pair", "panel"), None),
        P(("pair", "panel"), None),
        P("pair", "panel", None, None),
    )
    out_specs = P("pair", "panel")
    return jax.shard_map(
        on_device, mesh=mesh, in_specs=in_specs, out_specs=out_specs, check_vma=False
    )
```

profile of v0, /device:TPU:1, one launch (start us, length us, event | category | flops | bytes accessed | tf_op | source)
XLA Modules:
  0.0 165.6 jit_solution(11140317615342802263)
XLA Ops:
  6.5 0.0 copy-start
  6.5 0.0 all-gather.2.cloned.1.call-start
  6.5 2.1 %copy.25 = bf16[512,512]{0,1:T(8,128)(2,1)} copy(bf16[512,512]{1,0:T(8,128)(2,1)} %param.9) | data formatting | bytes 1048576 | tf_op args[0]
  8.7 0.0 all-gather.2.cloned.1.call-update
  8.7 0.7 fusion.10
  9.4 0.1 reduce_window_sum.11
  9.5 0.8 select_reduce_fusion
  10.4 0.7 convert_bitcast_fusion.1
  11.0 0.7 and_reduce_fusion
  11.7 1.0 scatter_custom_fusion.1
  12.7 0.8 all_to_all.16
  13.5 14.5 %all-to-all-start.1 = ((bf16[64,1,2]{2,1,0:T(2,128)(2,1)}), bf16[64,1,2]{2,1,0:T(2,128)(2,1)S(1)}, u32[]{:S(2)}, u32[]{:S(2)}) async-start(bf16[64,1,2]{2,1,0:T(2,128)(2,1)} %all_to_all.16), calls=%async_computation.1 | async-start | bytes 65536 | tf_op jit(solution)/shard_map/all_to_all | solution.py:67
  28.0 1.2 reshape.144
  29.2 0.1 copy.30
  29.3 1.1 broadcast_in_dim.53
  30.4 7.1 %scatter_fusion = bf16[128,32,128]{2,1,0:T(8,128)(2,1)} fusion(bf16[128,32,128]{2,1,0:T(8,128)(2,1)} %broadcast_in_dim.53, s32[64]{0:T(128)S(1)} %bitcast.71, bf16[64,32,128]{2,1,0:T(8,128)(2,1)S(1)} %bitcast.61), kind=kCustom, calls=%fused_computation.3 | custom fusion | bytes 1573120 | tf_op jit(solution)/shard_map/scatter | solution.py:56
  37.5 0.0 all-to-all-done.1
  37.5 10.4 %all-to-all-start = ((bf16[64,2,32,128]{3,2,1,0:T(8,128)(2,1)}), bf16[64,2,32,128]{3,2,1,0:T(8,128)(2,1)S(1)}, u32[]{:S(2)}, u32[]{:S(2)}) async-start(bf16[64,2,32,128]{3,2,1,0:T(8,128)(2,1)} %bitcast.14), calls=%async_computation | async-start | bytes 2097152 | tf_op jit(solution)/shard_map/all_to_all | solution.py:66
  48.0 0.1 reshape.151
  48.1 0.1 convert_reduce_fusion
  48.2 0.1 reshape.150
  48.4 0.0 copy-done
  48.4 3.1 %gather_fusion.1 = bf16[128,128,128]{2,1,0:T(8,128)(2,1)} fusion(bf16[16,128,128]{2,1,0:T(8,128)(2,1)S(1)} %bitcast.54, s32[1024]{0:T(1024)S(1)} %pad_clamp_fusion.1), kind=kCustom, calls=%fused_computation.1 | custom fusion | bytes 8389120 | tf_op jit(solution)/shard_map/jit(_take)/gather | solution.py:69
  51.5 24.4 %all-to-all-done = bf16[64,2,32,128]{3,2,1,0:T(8,128)(2,1)S(1)} async-done(((bf16[64,2,32,128]{3,2,1,0:T(8,128)(2,1)}), bf16[64,2,32,128]{3,2,1,0:T(8,128)(2,1)S(1)}, u32[]{:S(2)}, u32[]{:S(2)}) %all-to-all-start) | async-done | bytes 1048608 | tf_op jit(solution)/shard_map/all_to_all | solution.py:66
  75.9 0.0 copy-start.2
  75.9 4.5 %fusion.6 = bf16[128,32,128]{2,1,0:T(8,128)(2,1)} fusion(bf16[128,32,128]{2,1,0:T(8,128)(2,1)S(1)} %bitcast.64, bf16[128,128,128]{2,1,0:T(8,128)(2,1)} %gather_fusion.1, pred[128]{0:T(512)(128)(4,1)S(1)} %compare_and_fusion), kind=kOutput, calls=%fused_computation.12 | convolution fusion | flops 136839168 | bytes 6291584 | tf_op jit(solution)/shard_map/src,scd->srd/dot_general | solution.py:71
  80.4 0.0 copy-start.5
  80.4 6.8 %all-to-all-start.2 = ((bf16[64,2,32,128]{3,2,1,0:T(8,128)(2,1)}), bf16[64,2,32,128]{3,2,1,0:T(8,128)(2,1)}, u32[]{:S(2)}, u32[]{:S(2)}) async-start(bf16[64,2,32,128]{3,2,1,0:T(8,128)(2,1)} %bitcast.19), calls=%async_computation.2 | async-start | bytes 2097152 | tf_op jit(solution)/shard_map/all_to_all | solution.py:74
  87.2 0.1 broadcast_in_dim.51
  87.3 0.0 copy-done.2
  87.3 0.1 reshape_squeeze.10
  87.4 0.1 broadcast_bitcast_fusion
  87.5 3.0 %copy.24 = bf16[4,2048,128]{1,2,0:T(8,128)(2,1)S(1)} copy(bf16[4,2048,128]{2,1,0:T(8,128)(2,1)} %bitcast.60) | data formatting | bytes 4194304 | tf_op jit(solution)/shard_map/reshape;squeeze | solution.py:28
  90.5 0.0 copy-done.5
  90.5 0.1 fusion.11
  90.6 0.1 broadcast_bitcast_fusion.1
  90.7 24.4 %all-to-all-done.2 = bf16[64,2,32,128]{3,2,1,0:T(8,128)(2,1)} async-done(((bf16[64,2,32,128]{3,2,1,0:T(8,128)(2,1)}), bf16[64,2,32,128]{3,2,1,0:T(8,128)(2,1)}, u32[]{:S(2)}, u32[]{:S(2)}) %all-to-all-start.2) | async-done | bytes 1048608 | tf_op jit(solution)/shard_map/all_to_all | solution.py:74
  115.1 1.9 %gather_fusion.2 = bf16[64,32,128]{2,1,0:T(8,128)(2,1)S(1)} fusion(bf16[128,32,128]{2,1,0:T(8,128)(2,1)} %bitcast.20, s32[1024]{0:T(1024)S(1)} %pad_clamp_fusion), kind=kCustom, calls=%fused_computation.2 | custom fusion | bytes 1048832 | tf_op jit(solution)/shard_map/jit(_take)/gather | solution.py:77
  117.0 0.1 convert_bitcast_fusion
  117.2 1.7 %copy.32 = f32[16,32,4,128]{3,2,1,0:T(4,128)} copy(f32[16,32,4,128]{3,1,2,0:T(8,128)S(1)} %convert_bitcast_fusion) | data formatting | bytes 2097152 | tf_op jit(solution)/shard_map/convert_element_type | solution.py:84
  118.9 0.0 all-gather.2.cloned.1.call-done
  118.9 8.6 %copy.26 = bf16[512,48,128]{2,0,1:T(8,128)(2,1)} copy(bf16[512,48,128]{0,2,1:T(8,128)(2,1)} %bitcast.57) | data formatting | bytes 12582912 | tf_op jit(solution)/shard_map/reshape | solution.py:30
  127.4 8.3 %gather_fusion = bf16[64,512,128]{2,1,0:T(8,128)(2,1)} fusion(bf16[512,48,128]{2,0,1:T(8,128)(2,1)} %copy.26, s32[1024]{0:T(1024)S(1)} %pad_clamp_fusion.2), kind=kCustom, calls=%fused_computation | custom fusion | bytes 16777472 | tf_op jit(solution)/shard_map/jit(_take)/gather | solution.py:30
  135.7 11.9 %copy.27 = bf16[512,64,128]{0,2,1:T(8,128)(2,1)} copy(bf16[512,64,128]{2,0,1:T(8,128)(2,1)} %bitcast.55) | data formatting | bytes 16777216 | tf_op jit(solution)/shard_map/jit(_take)/gather | solution.py:30
  147.7 4.7 %bitcast_select_fusion = bf16[512,4,2048]{0,2,1:T(8,128)(2,1)S(1)} fusion(pred[4,2048]{1,0:T(4,128)(4,1)S(1)} %bitcast.67, bf16[512,4,2048]{0,2,1:T(8,128)(2,1)} %bitcast.56), kind=kLoop, calls=%fused_computation.5 | loop fusion | flops 4194304 | bytes 16785408 | tf_op jit(solution)/shard_map/jit(_take)/select_n | solution.py:30
  152.3 0.0 copy-start.1
  152.4 0.0 copy-start.3
  152.4 0.0 copy-start.4
  152.4 2.3 %fusion.4 = f32[4,128,512]{2,1,0:T(8,128)} fusion(bf16[512,4,2048]{0,2,1:T(8,128)(2,1)S(1)} %bitcast_select_fusion, bf16[4,2048,128]{1,2,0:T(8,128)(2,1)S(1)} %copy.24, bf16[4,2048]{1,0:T(4,128)(2,1)S(1)} %bitcast.65), kind=kOutput, calls=%fused_computation.10 | convolution fusion | flops 1074790400 | bytes 11550720 | tf_op jit(solution)/shard_map/rkc,kcd->rkd/dot_general | solution.py:32
  154.7 1.6 copy.29
  156.3 0.0 copy-done.1
  156.3 0.0 copy-done.3
  156.3 0.0 copy-done.4
  156.3 2.4 %bitcast_add_fusion = f32[512,512]{1,0:T(8,128)} fusion(f32[64,8,4,128]{3,2,1,0:T(4,128)} %bitcast.58, f32[512,512]{1,0:T(8,128)S(1)} %copy.29, bf16[512,512]{1,0:T(8,128)(2,1)S(1)} %copy-done.1, f32[512]{0:T(512)S(1)} %copy-done.3, f32[512]{0:T(512)S(1)} %copy-done.4), kind=kLoop, calls=%fused_computation.13 | loop fusion | flops 1310720 | bytes 3674112 | tf_op jit(solution)/shard_map/add | solution.py:84
  (10 shorter events, 0.1 us)
Async XLA Ops:
  6.5 41.9 %copy-start = (bf16[1,16,128,128]{3,2,1,0:T(8,128)(2,1)S(1)}, bf16[1,16,128,128]{3,2,1,0:T(8,128)(2,1)}, u32[]{:S(2)}) copy-start(bf16[1,16,128,128]{3,2,1,0:T(8,128)(2,1)} %param.17) | copy-start | bytes 1572868
  6.5 112.3 %all-gather.2.cloned.1.call-start = ((), (), s32[]{:S(2)}) async-start(), calls=%async_computation.3 | async-start | bytes 6815744 | tf_op jit(solution)/shard_map/all_gather | solution.py:29
  13.5 24.1 %all-to-all-start.1 = ((bf16[64,1,2]{2,1,0:T(2,128)(2,1)}), bf16[64,1,2]{2,1,0:T(2,128)(2,1)S(1)}, u32[]{:S(2)}, u32[]{:S(2)}) async-start(bf16[64,1,2]{2,1,0:T(2,128)(2,1)} %all_to_all.16), calls=%async_computation.1 | async-start | bytes 65536 | tf_op jit(solution)/shard_map/all_to_all | solution.py:67
  37.5 38.4 %all-to-all-start = ((bf16[64,2,32,128]{3,2,1,0:T(8,128)(2,1)}), bf16[64,2,32,128]{3,2,1,0:T(8,128)(2,1)S(1)}, u32[]{:S(2)}, u32[]{:S(2)}) async-start(bf16[64,2,32,128]{3,2,1,0:T(8,128)(2,1)} %bitcast.14), calls=%async_computation | async-start | bytes 2097152 | tf_op jit(solution)/shard_map/all_to_all | solution.py:66
  75.9 11.4 %copy-start.2 = (s32[1,4,16]{2,1,0:T(4,128)S(1)}, s32[1,4,16]{2,1,0:T(4,128)}, u32[]{:S(2)}) copy-start(s32[1,4,16]{2,1,0:T(4,128)} %param.12) | copy-start | bytes 772
  80.4 10.1 %copy-start.5 = (s32[1,4]{1,0:T(1,128)S(1)}, s32[1,4]{1,0:T(1,128)}, u32[]{:S(2)}) copy-start(s32[1,4]{1,0:T(1,128)} %param.13) | copy-start | bytes 52
  80.4 34.7 %all-to-all-start.2 = ((bf16[64,2,32,128]{3,2,1,0:T(8,128)(2,1)}), bf16[64,2,32,128]{3,2,1,0:T(8,128)(2,1)}, u32[]{:S(2)}, u32[]{:S(2)}) async-start(bf16[64,2,32,128]{3,2,1,0:T(8,128)(2,1)} %bitcast.19), calls=%async_computation.2 | async-start | bytes 2097152 | tf_op jit(solution)/shard_map/all_to_all | solution.py:74
  152.3 3.9 %copy-start.1 = (bf16[512,512]{1,0:T(8,128)(2,1)S(1)}, bf16[512,512]{1,0:T(8,128)(2,1)}, u32[]{:S(2)}) copy-start(bf16[512,512]{1,0:T(8,128)(2,1)} %param.9) | copy-start | bytes 1572868
  152.4 3.9 %copy-start.3 = (f32[512]{0:T(512)S(1)}, f32[512]{0:T(512)}, u32[]{:S(2)}) copy-start(f32[512]{0:T(512)} %param.10) | copy-start | bytes 6148
  152.4 3.9 %copy-start.4 = (f32[512]{0:T(512)S(1)}, f32[512]{0:T(512)}, u32[]{:S(2)}) copy-start(f32[512]{0:T(512)} %param.11) | copy-start | bytes 6148
Sparse Core Ops, SparseCore 0:
  9.7 92.0 all-gather.1
where the time goes:
time: 167 us; the launch traced here: 166 us
  local copies, waits for them, and re-layouts  54.1 us (32%)
  waiting for transfers between devices  48.8 us (29%)
  starting transfers between devices  31.7 us (19%)
  between operations  13.6 us (8%)
  other arithmetic  10.5 us (6%)
  matrix products  6.84 us (4%)
    all_to_all x1, waiting for transfers between devices, on_device(): lax.all_to_all(product.reshape(got_tiles.shape), 'pair', split_axis=0, co...  24.4 us
    all_to_all x1, waiting for transfers between devices, on_device(): lax.all_to_all(send_tiles, 'pair', split_axis=0, concat_axis=0, tiled=True)  24.4 us
    gather x2, local copies, waits for them, and re-layouts, on_device(): jnp.take(gathered.reshape(slab_rows, all_tiles, TB), lists.reshape(-1), a...  20.2 us
    all_to_all x1, starting transfers between devices, on_device(): lax.all_to_all(send_index, 'pair', split_axis=0, concat_axis=0, tiled=True)  14.5 us
    all_to_all x1, starting transfers between devices, on_device(): lax.all_to_all(send_tiles, 'pair', split_axis=0, concat_axis=0, tiled=True)  10.4 us
    reshape x1, local copies, waits for them, and re-layouts, on_device(): gathered.reshape(slab_rows, all_tiles, TB)  8.57 us
    scatter x1, local copies, waits for them, and re-layouts, on_device(): jnp.zeros((pair_count * capacity, RR, TB), jnp.bfloat16).at[position]  7.15 us
    all_to_all x1, starting transfers between devices, on_device(): lax.all_to_all(product.reshape(got_tiles.shape), 'pair', split_axis=0, co...  6.79 us
  transfers between devices with their start and end apart: 4, of which 2 were waited for; matrix products, arithmetic and copies ran while one was open for 17% of the time, Pallas kernels for 0%

commit v1 on v0

v1 whole, which is shorter than its diff:
```python
import functools

import jax
import jax.numpy as jnp
from jax import lax
from jax.experimental import pallas as pl
from jax.experimental.pallas import tpu as pltpu
from jax.sharding import PartitionSpec as P

TB = 128
LMAX = 16
RR = 32
CAP = 2
KP = 4
MESH = pl.DeviceIdType.MESH

FIRST = 5
GROUP = 8


def kernel(
    n_pair,
    n_panel,
    inv_ref,
    source_ref,
    place_ref,
    amps_ref,
    pair_energy_ref,
    virt_energy_ref,
    slot_ref,
    ladder_hbm,
    cycle_hbm,
    out_ref,
    ladder_ref,
    cycle_ref,
    held,
    own,
    mats,
    send,
    got,
    prod,
    ret,
    got_slot,
    slot_table,
    local_sem,
    right_send,
    right_recv,
    left_send,
    left_recv,
    tile_send,
    tile_recv,
    slot_send,
    slot_recv,
    back_send,
    back_recv,
):
    p = lax.axis_index("pair")
    q = lax.axis_index("panel")
    right = (p, lax.rem(q + 1, n_panel))
    left = (p, lax.rem(q + n_panel - 1, n_panel))
    slab = amps_ref.shape[0]
    row_tiles = slab // RR
    half = n_panel // 2
    steps = KP * (half - 1) + KP // 2

    load_ladder = pltpu.make_async_copy(ladder_hbm, ladder_ref, local_sem.at[0])
    load_cycle = pltpu.make_async_copy(cycle_hbm, cycle_ref, local_sem.at[1])
    load_ladder.start()
    load_cycle.start()

    barrier = pltpu.get_barrier_semaphore()
    for neighbour in (left, right):
        pl.semaphore_signal(barrier, inc=1, device_id=neighbour, device_id_type=MESH)

    def greet(d, carry):
        pl.semaphore_signal(
            barrier, inc=1, device_id=(lax.rem(p + d, n_pair), q), device_id_type=MESH
        )
        return carry

    lax.fori_loop(1, n_pair, greet, 0)
    pl.semaphore_wait(barrier, n_pair + 1)

    def to_right(source, tile, s):
        return pltpu.make_async_remote_copy(
            src_ref=source,
            dst_ref=held.at[tile],
            send_sem=right_send.at[s],
            recv_sem=right_recv.at[s],
            device_id=right,
            device_id_type=MESH,
        )

    def to_left(source, tile, s):
        return pltpu.make_async_remote_copy(
            src_ref=source,
            dst_ref=held.at[tile],
            send_sem=left_send.at[s],
            recv_sem=left_recv.at[s],
            device_id=left,
            device_id_type=MESH,
        )

    for s in range(KP):
        j, k = s, (s + KP // 2) % KP
        to_right(amps_ref.at[:, pl.ds(j * TB, TB)], q * KP + j, s).start()
        to_left(amps_ref.at[:, pl.ds(k * TB, TB)], q * KP + k, s).start()

    for r in range(row_tiles):
        for k in range(KP):
            own[r * KP + k] = amps_ref[pl.ds(r * RR, RR), pl.ds(k * TB, TB)]

    def dispatch(d, carry):
        peer = lax.rem(p + d, n_pair)
        for c in range(CAP):
            send[peer, c] = own[source_ref[0, peer * CAP + c]]
        pltpu.make_async_remote_copy(
            src_ref=send.at[peer],
            dst_ref=got.at[p],
            send_sem=tile_send,
            recv_sem=tile_recv.at[p],
            device_id=(peer, q),
            device_id_type=MESH,
        ).start()
        pltpu.make_async_remote_copy(
            src_ref=slot_ref,
            dst_ref=got_slot.at[p],
            send_sem=slot_send,
            recv_sem=slot_recv,
            device_id=(peer, q),
            device_id_type=MESH,
        ).start()
        return carry

    lax.fori_loop(1, n_pair, dispatch, 0)
    for c in range(CAP):
        got[p, c] = own[source_ref[0, p * CAP + c]]
    got_slot[p] = slot_ref[...]

    for b in range(slab // TB):
        rows = pl.ds(b * TB, TB)
        column = jnp.transpose(
            jnp.broadcast_to(pair_energy_ref[:, rows], (TB, TB)), (1, 0)
        )
        for k in range(KP):
            cols = pl.ds(k * TB, TB)
            out_ref[rows, cols] = (virt_energy_ref[:, cols] - column) * amps_ref[
                rows, cols
            ].astype(jnp.float32)

    load_ladder.wait()
    load_cycle.wait()

    def add_ladder(first, second, first_tile, second_tile):
        for i, tile in enumerate((first_tile, second_tile)):
            for k in range(KP):
                entry = inv_ref[k, tile]
                mat = ladder_ref[k * LMAX + jnp.maximum(entry - 1, 0)]
                mats[pl.ds(i * TB, TB), pl.ds(k * TB, TB)] = jnp.where(
                    entry > 0, mat, jnp.zeros_like(mat)
                )
        lhs = jnp.concatenate([first, second], axis=1)
        for n in range(KP // 2):
            cols = pl.ds(n * 2 * TB, 2 * TB)
            out_ref[:, cols] += jnp.dot(
                lhs, mats[:, cols], preferred_element_type=jnp.float32
            )

    for j in range(0, KP, 2):
        add_ladder(
            amps_ref[:, pl.ds(j * TB, TB)],
            amps_ref[:, pl.ds((j + 1) * TB, TB)],
            q * KP + j,
            q * KP + j + 1,
        )

    def ring(s):
        hop = s // KP + 1
        from_left = lax.rem(q + n_panel - hop, n_panel) * KP + lax.rem(s, KP)
        from_right = lax.rem(q + hop, n_panel) * KP + lax.rem(s + KP // 2, KP)
        to_right(held.at[from_left], from_left, s).wait_recv()

        @pl.when(s < steps - KP)
        def _():
            to_right(held.at[from_left], from_left, s + KP).start()

        to_left(held.at[from_right], from_right, s).wait_recv()

        @pl.when(s < steps - KP)
        def _():
            to_left(held.at[from_right], from_right, s + KP).start()

        add_ladder(held[from_left], held[from_right], from_left, from_right)

    def back(source, s):
        return pltpu.make_async_remote_copy(
            src_ref=prod.at[source],
            dst_ref=ret.at[p],
            send_sem=back_send,
            recv_sem=back_recv,
            device_id=(source, q),
            device_id_type=MESH,
        )

    def multiply(source):
        for c in range(CAP):
            mat = cycle_ref[slot_table[source, 0, p * CAP + c]]
            prod[source, c] = jnp.dot(
                got[source, c], mat, preferred_element_type=jnp.float32
            ).astype(jnp.bfloat16)

    def answer(base, count):
        sources = [lax.rem(p + n_pair - (base + u), n_pair) for u in range(count)]
        for source in sources:
            pltpu.make_async_remote_copy(
                src_ref=send.at[source],
                dst_ref=got.at[source],
                send_sem=tile_send,
                recv_sem=tile_recv.at[source],
                device_id=(source, q),
                device_id_type=MESH,
            ).wait_recv()
        for source in sources:
            multiply(source)
        for source in sources:
            back(source, 0).start()

    others = n_pair - 1
    group = min(GROUP, others)
    chunks = others // group
    rest = others - chunks * group
    first = min(FIRST, max(0, steps - chunks))

    def plain(s, carry):
        ring(s)
        return carry

    def both(s, carry):
        ring(s)
        answer(1 + (s - first) * group, group)
        return carry

    lax.fori_loop(0, first, plain, 0)
    all_slots = pltpu.make_async_remote_copy(
        src_ref=got_slot.at[pl.ds(0, others)],
        dst_ref=got_slot.at[pl.ds(0, others)],
        send_sem=slot_send,
        recv_sem=slot_recv,
        device_id=right,
        device_id_type=MESH,
    )
    all_slots.wait_recv()
    to_table = pltpu.make_async_copy(got_slot, slot_table, local_sem.at[2])
    to_table.start()
    to_table.wait()
    lax.fori_loop(first, first + chunks, both, 0)
    if rest:
        answer(1 + chunks * group, rest)
    multiply(p)
    ret[p] = prod[p]
    lax.fori_loop(first + chunks, steps, plain, 0)

    all_back = pltpu.make_async_remote_copy(
        src_ref=prod.at[pl.ds(0, others)],
        dst_ref=ret.at[pl.ds(0, others)],
        send_sem=back_send,
        recv_sem=back_recv,
        device_id=right,
        device_id_type=MESH,
    )
    all_back.wait_recv()
    for r in range(row_tiles):
        for k in range(KP):
            place = place_ref[0, r * KP + k]
            out_ref[pl.ds(r * RR, RR), pl.ds(k * TB, TB)] += ret[
                place // CAP, lax.rem(place, CAP)
            ].astype(jnp.float32)

    def sent(s, carry):
        to_right(held.at[0], 0, s).wait_send()
        to_left(held.at[0], 0, s).wait_send()
        return carry

    lax.fori_loop(0, steps, sent, 0)
    all_slots.wait_send()
    all_back.wait_send()
    pltpu.make_async_remote_copy(
        src_ref=send.at[pl.ds(0, others)],
        dst_ref=got.at[pl.ds(0, others)],
        send_sem=tile_send,
        recv_sem=back_recv,
        device_id=right,
        device_id_type=MESH,
    ).wait_send()


def on_device(
    n_pair,
    n_panel,
    amps,
    pair_energy,
    virt_energy,
    ladder_rows,
    ladder_count,
    ladder_tiles,
    cycle_owner,
    cycle_slot,
    cycle_tiles,
):
    slab = amps.shape[0]
    tiles = cycle_owner.shape[0]
    steps = KP * (n_panel // 2 - 1) + KP // 2

    lists = ladder_rows[0]
    live = lax.broadcasted_iota(jnp.int32, (KP, LMAX), 1) < ladder_count[0][:, None]
    names = lax.broadcasted_iota(jnp.int32, (KP, LMAX, n_panel * KP), 2)
    order = lax.broadcasted_iota(jnp.int32, (KP, LMAX, n_panel * KP), 1) + 1
    hit = (lists[:, :, None] == names) & live[:, :, None]
    inv = jnp.max(jnp.where(hit, order, 0), axis=1)

    owner = cycle_owner[:, 0]
    code = lax.broadcasted_iota(jnp.int32, (tiles,), 0) * 16 + cycle_slot[:, 0]
    hot = owner[:, None] == lax.broadcasted_iota(jnp.int32, (tiles, n_pair), 1)
    top = tiles * 16 - 1
    low = jnp.min(jnp.where(hot, code[:, None], top), axis=0)
    high = jnp.max(jnp.where(hot, code[:, None], 0), axis=0)
    codes = jnp.stack([low, high], axis=1).reshape(1, n_pair * CAP)
    source = codes // 16
    slots = codes % 16
    same = owner[:, None] == owner[None, :]
    before = lax.broadcasted_iota(jnp.int32, (tiles, tiles), 0) < lax.broadcasted_iota(
        jnp.int32, (tiles, tiles), 1
    )
    second = jnp.any(same & before, axis=0).astype(jnp.int32)
    place = (owner * CAP + second).reshape(1, tiles)

    smem = pl.BlockSpec(memory_space=pltpu.SMEM)
    vmem = pl.BlockSpec(memory_space=pltpu.VMEM)
    anyspace = pl.BlockSpec(memory_space=pl.ANY)
    dma = pltpu.SemaphoreType.DMA
    return pl.pallas_call(
        functools.partial(kernel, n_pair, n_panel),
        out_shape=jax.ShapeDtypeStruct((slab, KP * TB), jnp.float32),
        in_specs=[smem] * 3 + [vmem] * 4 + [anyspace] * 2,
        out_specs=vmem,
        scratch_shapes=[
            pltpu.VMEM((KP * LMAX, TB, TB), jnp.bfloat16),
            pltpu.VMEM((cycle_tiles.shape[1], TB, TB), jnp.bfloat16),
            pltpu.VMEM((n_panel * KP, slab, TB), jnp.bfloat16),
            pltpu.VMEM((tiles, RR, TB), jnp.bfloat16),
            pltpu.VMEM((2 * TB, KP * TB), jnp.bfloat16),
            pltpu.VMEM((n_pair, CAP, RR, TB), jnp.bfloat16),
            pltpu.VMEM((n_pair, CAP, RR, TB), jnp.bfloat16),
            pltpu.VMEM((n_pair, CAP, RR, TB), jnp.bfloat16),
            pltpu.VMEM((n_pair, CAP, RR, TB), jnp.bfloat16),
            pltpu.VMEM((n_pair, 1, n_pair * CAP), jnp.int32),
            pltpu.SMEM((n_pair, 1, n_pair * CAP), jnp.int32),
            dma((3,)),
            dma((steps,)),
            dma((steps,)),
            dma((steps,)),
            dma((steps,)),
            dma(()),
            dma((n_pair,)),
            dma(()),
            dma(()),
            dma(()),
            dma(()),
        ],
        compiler_params=pltpu.CompilerParams(
            collective_id=0, has_side_effects=True, vmem_limit_bytes=40 * 1024 * 1024
        ),
        cost_estimate=pl.CostEstimate(
            flops=4 * 10**9, bytes_accessed=5 * 10**6, transcendentals=0
        ),
    )(
        inv,
        source,
        place,
        amps,
        pair_energy.reshape(1, slab),
        virt_energy.reshape(1, KP * TB),
        slots,
        ladder_tiles[0],
        cycle_tiles[0],
    )


def solution(mesh):
    in_specs = (
        P("pair", "panel"),
        P("pair"),
        P("panel"),
        P("pair", "panel", None),
        P("pair", "panel"),
        P("pair", "panel", None, None),
        P(("pair", "panel"), None),
        P(("pair", "panel"), None),
        P("pair", "panel", None, None),
    )
    return jax.shard_map(
        functools.partial(on_device, mesh.shape["pair"], mesh.shape["panel"]),
        mesh=mesh,
        in_specs=in_specs,
        out_specs=P("pair", "panel"),
        check_vma=False,
    )
```

time: 167 us -> 101 us (0.60)
  Pallas kernels: 0 us -> 88.8 us
  waiting for transfers between devices: 48.8 us -> 0 us
  local copies, waits for them, and re-layouts: 54.1 us -> 6.24 us
  starting transfers between devices: 31.7 us -> 0 us
  between operations: 13.6 us -> 0.05 us
  matrix products: 6.84 us -> 0 us
  other arithmetic: 10.5 us -> 4.42 us
    pallas_call x0 -> x1, Pallas kernels: none -> 88.8 us  [on_device(): pl.pallas_call(functools.partial(kernel, n_pair, n_panel), out_shape=jax....]
    all_to_all x3 -> x0, waiting for transfers between devices: 48.8 us -> none  [the longest x1 24.4 us: on_device(): lax.all_to_all(product.reshape(got_tiles.shape), 'pair', split_axis=0, co...]
    all_to_all x3 -> x0, starting transfers between devices: 31.7 us -> none  [the longest x1 14.5 us: on_device(): lax.all_to_all(send_index, 'pair', split_axis=0, concat_axis=0, tiled=True)]
    gather x4 -> x0, local copies, waits for them, and re-layouts: 25.2 us -> none  [the longest x2 20.2 us: on_device(): jnp.take(gathered.reshape(slab_rows, all_tiles, TB), lists.reshape(-1), a...]
    reshape x3 -> x1, local copies, waits for them, and re-layouts: 11.3 us -> 0.14 us  [on_device(): codes = jnp.stack([low, high], axis=1).reshape(1, n_pair * CAP)]
    scatter x2 -> x0, local copies, waits for them, and re-layouts: 8.1 us -> none  [the longest x1 7.15 us: on_device(): jnp.zeros((pair_count * capacity, RR, TB), jnp.bfloat16).at[position]]
    dot_general x2 -> x0, matrix products: 6.84 us -> none  [the longest x1 4.5 us: on_device(): jnp.einsum('src,scd->srd', flat_tiles, mats, preferred_element_type=jnp.f...]
    select_n x3 -> x1, other arithmetic: 4.68 us -> 0.01 us  [on_device(): slots = codes % 16]
  transfers between devices with their start and end apart: 4 -> 0, of which waited for: 2 -> 0; matrix products, arithmetic and copies ran while one was open for 17% -> 0% of each run, Pallas kernels for 0% -> 0%
where the time goes in v1:
time: 101 us; the launch traced here: 99.5 us
  Pallas kernels  88.8 us (88%)
  local copies, waits for them, and re-layouts  6.24 us (6%)
  other arithmetic  4.42 us (4%)
    pallas_call x1, Pallas kernels, on_device(): pl.pallas_call(functools.partial(kernel, n_pair, n_panel), out_shape=jax....  88.8 us
    unnamed x11, local copies, waits for them, and re-layouts  6 us

profile of v1, /device:TPU:1, one launch (start us, length us, event | category | flops | bytes accessed | tf_op | source)
XLA Modules:
  0.0 99.5 jit_solution(15803473296908950351)
XLA Ops:
  0.0 0.7 iota_compare_fusion.3
  0.7 0.7 add_bitcast_fusion
  1.4 0.8 fusion.2
  2.2 0.7 bitcast_add_fusion.place_ref
  2.9 0.7 select_reduce_fusion.1
  3.6 0.8 select_reduce_fusion.2.inv_ref
  4.4 0.1 copy.12
  4.5 0.1 reshape.205
  4.7 0.0 copy-start
  4.7 1.6 %copy-done = bf16[1,64,128,128]{3,2,1,0:T(8,128)(2,1)S(1)} copy-done((bf16[1,64,128,128]{3,2,1,0:T(8,128)(2,1)S(1)}, bf16[1,64,128,128]{3,2,1,0:T(8,128)(2,1)}, u32[]{:S(2)}) %copy-start) | copy-done | bytes 2097176
  6.3 0.0 copy-start.1
  6.3 1.0 %copy-done.1 = bf16[512,512]{1,0:T(8,128)(2,1)S(1)} copy-done((bf16[512,512]{1,0:T(8,128)(2,1)S(1)}, bf16[512,512]{1,0:T(8,128)(2,1)}, u32[]{:S(2)}) %copy-start.1) | copy-done | bytes 524312
  7.3 0.0 copy-start.2
  7.3 1.0 %copy-done.2 = bf16[1,16,128,128]{3,2,1,0:T(8,128)(2,1)S(1)} copy-done((bf16[1,16,128,128]{3,2,1,0:T(8,128)(2,1)S(1)}, bf16[1,16,128,128]{3,2,1,0:T(8,128)(2,1)}, u32[]{:S(2)}) %copy-start.2) | copy-done | bytes 524312
  8.4 0.0 copy-start.3
  8.4 0.7 copy-done.3
  9.0 0.0 copy-start.4
  9.0 0.7 copy-done.4
  9.7 88.8 %shard_map.91 = f32[512,512]{1,0:T(8,128)S(1)} custom-call(s32[4,48]{1,0:T(4,128)S(1)} %select_reduce_fusion.2.inv_ref, s32[1,128]{1,0:T(1,128)S(1)} %get-tuple-element.8.source_ref, s32[1,64]{1,0:T(1,128)S(1)} %bitcast_add_fusion.place_ref, bf16[512,512]{1,0:T(8,128)(2,1)S(1)} %copy-done.1, f32[1,512]{1,0:T(1,128)S(1)} %bitcast.17, f32[1,512]{1,0:T(1,128)S(1)} %bitcast.18, ...), custom_call_target="tpu_custom_call" | custom-call | flops 4000000000 | bytes 5000000 | tf_op jit(solution)/shard_map/pallas_call | solution.py:341
  98.5 1.0 copy.14
  (3 shorter events, 0.0 us)
Async XLA Ops:
  4.7 1.6 %copy-start = (bf16[1,64,128,128]{3,2,1,0:T(8,128)(2,1)S(1)}, bf16[1,64,128,128]{3,2,1,0:T(8,128)(2,1)}, u32[]{:S(2)}) copy-start(bf16[1,64,128,128]{3,2,1,0:T(8,128)(2,1)} %param.14) | copy-start | bytes 6291460
  6.3 1.0 %copy-start.1 = (bf16[512,512]{1,0:T(8,128)(2,1)S(1)}, bf16[512,512]{1,0:T(8,128)(2,1)}, u32[]{:S(2)}) copy-start(bf16[512,512]{1,0:T(8,128)(2,1)} %amps_ref.1) | copy-start | bytes 1572868
  7.3 1.0 %copy-start.2 = (bf16[1,16,128,128]{3,2,1,0:T(8,128)(2,1)S(1)}, bf16[1,16,128,128]{3,2,1,0:T(8,128)(2,1)}, u32[]{:S(2)}) copy-start(bf16[1,16,128,128]{3,2,1,0:T(8,128)(2,1)} %param.17) | copy-start | bytes 1572868
  8.4 0.7 copy-start.3
  9.0 0.7 copy-start.4

commit v2 on v1

--- a/solution.py
+++ b/solution.py
@@ -11,25 +11,39 @@
 LMAX = 16
 RR = 32
 CAP = 2
+SLOTS = 16
+CODES = 1024
 KP = 4
 MESH = pl.DeviceIdType.MESH
 
-FIRST = 5
-GROUP = 8
+FIRST = 7
+GROUP = 9
 
 
 def kernel(
     n_pair,
     n_panel,
+    owner_hbm,
+    slot_hbm,
+    lists_hbm,
+    count_hbm,
+    amps_hbm,
+    pair_energy_hbm,
+    virt_energy_hbm,
+    ladder_hbm,
+    cycle_hbm,
+    out_hbm,
+    owner_ref,
+    slot_ref,
+    lists_ref,
+    count_ref,
+    code_row,
+    inv_rows,
+    code_ref,
     inv_ref,
-    source_ref,
-    place_ref,
     amps_ref,
     pair_energy_ref,
     virt_energy_ref,
-    slot_ref,
-    ladder_hbm,
-    cycle_hbm,
     out_ref,
     ladder_ref,
     cycle_ref,
@@ -62,11 +76,26 @@
     row_tiles = slab // RR
     half = n_panel // 2
     steps = KP * (half - 1) + KP // 2
-
-    load_ladder = pltpu.make_async_copy(ladder_hbm, ladder_ref, local_sem.at[0])
-    load_cycle = pltpu.make_async_copy(cycle_hbm, cycle_ref, local_sem.at[1])
-    load_ladder.start()
-    load_cycle.start()
+    last = steps - 1
+
+    loads = [
+        pltpu.make_async_copy(source, target, local_sem.at[i])
+        for i, (source, target) in enumerate(
+            (
+                (amps_hbm, amps_ref),
+                (owner_hbm, owner_ref),
+                (slot_hbm, slot_ref),
+                (lists_hbm, lists_ref),
+                (count_hbm, count_ref),
+                (pair_energy_hbm, pair_energy_ref),
+                (virt_energy_hbm, virt_energy_ref),
+                (cycle_hbm, cycle_ref),
+                (ladder_hbm, ladder_ref),
+            )
+        )
+    ]
+    for load in loads:
+        load.start()
 
     barrier = pltpu.get_barrier_semaphore()
     for neighbour in (left, right):
@@ -79,6 +108,7 @@
         return carry
 
     lax.fori_loop(1, n_pair, greet, 0)
+    loads[0].wait()
     pl.semaphore_wait(barrier, n_pair + 1)
 
     def to_right(source, tile, s):
@@ -106,14 +136,49 @@
         to_right(amps_ref.at[:, pl.ds(j * TB, TB)], q * KP + j, s).start()
         to_left(amps_ref.at[:, pl.ds(k * TB, TB)], q * KP + k, s).start()
 
+    for load in loads[1:5]:
+        load.wait()
+    tiles = row_tiles * KP
+    lane = lax.broadcasted_iota(jnp.int32, (1, TB), 1)
+    low = jnp.zeros((1, TB), jnp.int32)
+    high = jnp.zeros((1, TB), jnp.int32)
+    for t in range(tiles):
+        u = tiles - 1 - t
+        high = jnp.where(lane == owner_ref[0, t], t * SLOTS + slot_ref[0, t], high)
+        low = jnp.where(lane == owner_ref[0, u], u * SLOTS + slot_ref[0, u], low)
+    code_row[...] = low * CODES + high
+    row = lax.broadcasted_iota(jnp.int32, (KP, TB), 0)
+    column = lax.broadcasted_iota(jnp.int32, (KP, TB), 1)
+    inv = jnp.zeros((KP, TB), jnp.int32)
+    for k in range(KP):
+        for i in range(LMAX):
+            named = jnp.where(i < count_ref[0, k], lists_ref[k, i], -1)
+            inv = jnp.where((row == k) & (column == named), i + 1, inv)
+    inv_rows[...] = inv
+    tables = [
+        pltpu.make_async_copy(code_row, code_ref, local_sem.at[9]),
+        pltpu.make_async_copy(inv_rows, inv_ref, local_sem.at[10]),
+    ]
+    for table in tables:
+        table.start()
+
     for r in range(row_tiles):
         for k in range(KP):
             own[r * KP + k] = amps_ref[pl.ds(r * RR, RR), pl.ds(k * TB, TB)]
 
+    for table in tables:
+        table.wait()
+
+    def codes_of(code):
+        return lax.shift_right_logical(code, 10), lax.bitwise_and(code, CODES - 1)
+
+    def fill(peer, target, place):
+        for c, code in enumerate(codes_of(code_ref[0, peer])):
+            target[place, c] = own[lax.shift_right_logical(code, 4)]
+
     def dispatch(d, carry):
         peer = lax.rem(p + d, n_pair)
-        for c in range(CAP):
-            send[peer, c] = own[source_ref[0, peer * CAP + c]]
+        fill(peer, send, peer)
         pltpu.make_async_remote_copy(
             src_ref=send.at[peer],
             dst_ref=got.at[p],
@@ -123,7 +188,7 @@
             device_id_type=MESH,
         ).start()
         pltpu.make_async_remote_copy(
-            src_ref=slot_ref,
+            src_ref=code_row,
             dst_ref=got_slot.at[p],
             send_sem=slot_send,
             recv_sem=slot_recv,
@@ -133,10 +198,11 @@
         return carry
 
     lax.fori_loop(1, n_pair, dispatch, 0)
-    for c in range(CAP):
-        got[p, c] = own[source_ref[0, p * CAP + c]]
-    got_slot[p] = slot_ref[...]
-
+    fill(p, got, p)
+    got_slot[p] = code_row[...]
+
+    for load in loads[5:]:
+        load.wait()
     for b in range(slab // TB):
         rows = pl.ds(b * TB, TB)
         column = jnp.transpose(
@@ -148,10 +214,7 @@
                 rows, cols
             ].astype(jnp.float32)
 
-    load_ladder.wait()
-    load_cycle.wait()
-
-    def add_ladder(first, second, first_tile, second_tile):
+    def pick(first_tile, second_tile):
         for i, tile in enumerate((first_tile, second_tile)):
             for k in range(KP):
                 entry = inv_ref[k, tile]
@@ -159,6 +222,8 @@
                 mats[pl.ds(i * TB, TB), pl.ds(k * TB, TB)] = jnp.where(
                     entry > 0, mat, jnp.zeros_like(mat)
                 )
+
+    def add_ladder(first, second):
         lhs = jnp.concatenate([first, second], axis=1)
         for n in range(KP // 2):
             cols = pl.ds(n * 2 * TB, 2 * TB)
@@ -167,20 +232,22 @@
             )
 
     for j in range(0, KP, 2):
+        pick(q * KP + j, q * KP + j + 1)
         add_ladder(
-            amps_ref[:, pl.ds(j * TB, TB)],
-            amps_ref[:, pl.ds((j + 1) * TB, TB)],
-            q * KP + j,
-            q * KP + j + 1,
-        )
-
-    def ring(s):
+            amps_ref[:, pl.ds(j * TB, TB)], amps_ref[:, pl.ds((j + 1) * TB, TB)]
+        )
+
+    def arrivals(s):
         hop = s // KP + 1
         from_left = lax.rem(q + n_panel - hop, n_panel) * KP + lax.rem(s, KP)
         from_right = lax.rem(q + hop, n_panel) * KP + lax.rem(s + KP // 2, KP)
+        return from_left, from_right
+
+    def ring(s):
+        from_left, from_right = arrivals(s)
         to_right(held.at[from_left], from_left, s).wait_recv()
 
-        @pl.when(s < steps - KP)
+        @pl.when((s < steps - KP) & ((s < last - KP) | (q != n_panel - 1)))
         def _():
             to_right(held.at[from_left], from_left, s + KP).start()
 
@@ -190,7 +257,12 @@
         def _():
             to_left(held.at[from_right], from_right, s + KP).start()
 
-        add_ladder(held[from_left], held[from_right], from_left, from_right)
+        @pl.when((s == steps - KP + 1) & (q == 1))
+        def _():
+            to_left(held.at[from_right], from_right, steps).start()
+
+        pick(from_left, from_right)
+        add_ladder(held[from_left], held[from_right])
 
     def back(source, s):
         return pltpu.make_async_remote_copy(
@@ -203,8 +275,8 @@
         )
 
     def multiply(source):
-        for c in range(CAP):
-            mat = cycle_ref[slot_table[source, 0, p * CAP + c]]
+        for c, code in enumerate(codes_of(slot_table[source, 0, p])):
+            mat = cycle_ref[lax.bitwise_and(code, SLOTS - 1)]
             prod[source, c] = jnp.dot(
                 got[source, c], mat, preferred_element_type=jnp.float32
             ).astype(jnp.bfloat16)
@@ -229,7 +301,7 @@
     group = min(GROUP, others)
     chunks = others // group
     rest = others - chunks * group
-    first = min(FIRST, max(0, steps - chunks))
+    first = min(FIRST, max(0, last - chunks))
 
     def plain(s, carry):
         ring(s)
@@ -250,7 +322,7 @@
         device_id_type=MESH,
     )
     all_slots.wait_recv()
-    to_table = pltpu.make_async_copy(got_slot, slot_table, local_sem.at[2])
+    to_table = pltpu.make_async_copy(got_slot, slot_table, local_sem.at[11])
     to_table.start()
     to_table.wait()
     lax.fori_loop(first, first + chunks, both, 0)
@@ -258,7 +330,7 @@
         answer(1 + chunks * group, rest)
     multiply(p)
     ret[p] = prod[p]
-    lax.fori_loop(first + chunks, steps, plain, 0)
+    lax.fori_loop(first + chunks, last, plain, 0)
 
     all_back = pltpu.make_async_remote_copy(
         src_ref=prod.at[pl.ds(0, others)],
@@ -271,17 +343,33 @@
     all_back.wait_recv()
     for r in range(row_tiles):
         for k in range(KP):
-            place = place_ref[0, r * KP + k]
-            out_ref[pl.ds(r * RR, RR), pl.ds(k * TB, TB)] += ret[
-                place // CAP, lax.rem(place, CAP)
-            ].astype(jnp.float32)
+            t = r * KP + k
+            owner = owner_ref[0, t]
+            first_code, _ = codes_of(code_ref[0, owner])
+            later = (lax.shift_right_logical(first_code, 4) != t).astype(jnp.int32)
+            out_ref[pl.ds(r * RR, RR), pl.ds(k * TB, TB)] += ret[owner, later].astype(
+                jnp.float32
+            )
+
+    from_left, from_right = arrivals(last)
+    pick(from_left, from_right)
 
     def sent(s, carry):
         to_right(held.at[0], 0, s).wait_send()
         to_left(held.at[0], 0, s).wait_send()
         return carry
 
-    lax.fori_loop(0, steps, sent, 0)
+    lax.fori_loop(0, last, sent, 0)
+    to_left(held.at[0], 0, last).wait_send()
+
+    @pl.when(q != n_panel - 1)
+    def _():
+        to_right(held.at[0], 0, last).wait_send()
+
+    @pl.when(q == 1)
+    def _():
+        to_left(held.at[0], 0, steps).wait_send()
+
     all_slots.wait_send()
     all_back.wait_send()
     pltpu.make_async_remote_copy(
@@ -292,6 +380,28 @@
         device_id=right,
         device_id_type=MESH,
     ).wait_send()
+
+    to_left(held.at[from_right], from_right, last).wait_recv()
+
+    @pl.when(q != 0)
+    def _():
+        to_right(held.at[from_left], from_left, last).wait_recv()
+
+    @pl.when(q == 0)
+    def _():
+        to_left(held.at[from_left], from_left, steps).wait_recv()
+
+    stores = []
+    for b in range(slab // TB):
+        rows = pl.ds(b * TB, TB)
+        lhs = jnp.concatenate([held[from_left, rows], held[from_right, rows]], axis=1)
+        out_ref[rows] += jnp.dot(lhs, mats[...], preferred_element_type=jnp.float32)
+        stores.append(
+            pltpu.make_async_copy(out_ref.at[rows], out_hbm.at[rows], local_sem.at[b])
+        )
+        stores[-1].start()
+    for store in stores:
+        store.wait()
 
 
 def on_device(
@@ -311,39 +421,26 @@
     tiles = cycle_owner.shape[0]
     steps = KP * (n_panel // 2 - 1) + KP // 2
 
-    lists = ladder_rows[0]
-    live = lax.broadcasted_iota(jnp.int32, (KP, LMAX), 1) < ladder_count[0][:, None]
-    names = lax.broadcasted_iota(jnp.int32, (KP, LMAX, n_panel * KP), 2)
-    order = lax.broadcasted_iota(jnp.int32, (KP, LMAX, n_panel * KP), 1) + 1
-    hit = (lists[:, :, None] == names) & live[:, :, None]
-    inv = jnp.max(jnp.where(hit, order, 0), axis=1)
-
-    owner = cycle_owner[:, 0]
-    code = lax.broadcasted_iota(jnp.int32, (tiles,), 0) * 16 + cycle_slot[:, 0]
-    hot = owner[:, None] == lax.broadcasted_iota(jnp.int32, (tiles, n_pair), 1)
-    top = tiles * 16 - 1
-    low = jnp.min(jnp.where(hot, code[:, None], top), axis=0)
-    high = jnp.max(jnp.where(hot, code[:, None], 0), axis=0)
-    codes = jnp.stack([low, high], axis=1).reshape(1, n_pair * CAP)
-    source = codes // 16
-    slots = codes % 16
-    same = owner[:, None] == owner[None, :]
-    before = lax.broadcasted_iota(jnp.int32, (tiles, tiles), 0) < lax.broadcasted_iota(
-        jnp.int32, (tiles, tiles), 1
-    )
-    second = jnp.any(same & before, axis=0).astype(jnp.int32)
-    place = (owner * CAP + second).reshape(1, tiles)
-
-    smem = pl.BlockSpec(memory_space=pltpu.SMEM)
-    vmem = pl.BlockSpec(memory_space=pltpu.VMEM)
     anyspace = pl.BlockSpec(memory_space=pl.ANY)
     dma = pltpu.SemaphoreType.DMA
     return pl.pallas_call(
         functools.partial(kernel, n_pair, n_panel),
         out_shape=jax.ShapeDtypeStruct((slab, KP * TB), jnp.float32),
-        in_specs=[smem] * 3 + [vmem] * 4 + [anyspace] * 2,
-        out_specs=vmem,
+        in_specs=[anyspace] * 9,
+        out_specs=anyspace,
         scratch_shapes=[
+            pltpu.SMEM((1, tiles), jnp.int32),
+            pltpu.SMEM((1, tiles), jnp.int32),
+            pltpu.SMEM((KP, LMAX), jnp.int32),
+            pltpu.SMEM((1, KP), jnp.int32),
+            pltpu.VMEM((1, TB), jnp.int32),
+            pltpu.VMEM((KP, TB), jnp.int32),
+            pltpu.SMEM((1, TB), jnp.int32),
+            pltpu.SMEM((KP, TB), jnp.int32),
+            pltpu.VMEM((slab, KP * TB), jnp.bfloat16),
+            pltpu.VMEM((1, slab), jnp.float32),
+            pltpu.VMEM((1, KP * TB), jnp.float32),
+            pltpu.VMEM((slab, KP * TB), jnp.float32),
             pltpu.VMEM((KP * LMAX, TB, TB), jnp.bfloat16),
             pltpu.VMEM((cycle_tiles.shape[1], TB, TB), jnp.bfloat16),
             pltpu.VMEM((n_panel * KP, slab, TB), jnp.bfloat16),
@@ -353,13 +450,13 @@
             pltpu.VMEM((n_pair, CAP, RR, TB), jnp.bfloat16),
             pltpu.VMEM((n_pair, CAP, RR, TB), jnp.bfloat16),
             pltpu.VMEM((n_pair, CAP, RR, TB), jnp.bfloat16),
-            pltpu.VMEM((n_pair, 1, n_pair * CAP), jnp.int32),
-            pltpu.SMEM((n_pair, 1, n_pair * CAP), jnp.int32),
-            dma((3,)),
+            pltpu.VMEM((n_pair, 1, TB), jnp.int32),
+            pltpu.SMEM((n_pair, 1, TB), jnp.int32),
+            dma((12,)),
             dma((steps,)),
             dma((steps,)),
-            dma((steps,)),
-            dma((steps,)),
+            dma((steps + 1,)),
+            dma((steps + 1,)),
             dma(()),
             dma((n_pair,)),
             dma(()),
@@ -368,19 +465,19 @@
             dma(()),
         ],
         compiler_params=pltpu.CompilerParams(
-            collective_id=0, has_side_effects=True, vmem_limit_bytes=40 * 1024 * 1024
+            collective_id=0, has_side_effects=True, vmem_limit_bytes=60 * 1024 * 1024
         ),
         cost_estimate=pl.CostEstimate(
             flops=4 * 10**9, bytes_accessed=5 * 10**6, transcendentals=0
         ),
     )(
-        inv,
-        source,
-        place,
+        cycle_owner.reshape(1, tiles),
+        cycle_slot.reshape(1, tiles),
+        ladder_rows[0],
+        ladder_count,
         amps,
         pair_energy.reshape(1, slab),
         virt_energy.reshape(1, KP * TB),
-        slots,
         ladder_tiles[0],
         cycle_tiles[0],
     )

time: 101 us -> 88.7 us (0.88); the launches traced: 99.5 us -> 88.6 us
  other arithmetic: 4.42 us -> 0 us
  local copies, waits for them, and re-layouts: 6.24 us -> 2.26 us
  Pallas kernels: 88.8 us -> 86.3 us
    unnamed x11 -> x1, local copies, waits for them, and re-layouts: 6 us -> 2.26 us
    pallas_call x1, Pallas kernels: 88.8 us -> 86.3 us  [on_device(): pl.pallas_call(functools.partial(kernel, n_pair, n_panel), out_shape=jax....]
where the time goes in v2:
time: 88.7 us; the launch traced here: 88.6 us
  Pallas kernels  86.3 us (97%)
  local copies, waits for them, and re-layouts  2.26 us (3%)
    pallas_call x1, Pallas kernels, on_device(): pl.pallas_call(functools.partial(kernel, n_pair, n_panel), out_shape=jax....  86.3 us
    unnamed x1, local copies, waits for them, and re-layouts  2.26 us

profile of v2, /device:TPU:1, one launch (start us, length us, event | category | flops | bytes accessed | tf_op | source)
XLA Modules:
  0.0 88.6 jit_solution(2212146006648250238)
XLA Ops:
  0.0 86.3 %shard_map.91 = f32[512,512]{1,0:T(8,128)} custom-call(s32[1,64]{1,0:T(1,128)} %bitcast.12, s32[1,64]{1,0:T(1,128)} %bitcast.13, s32[4,16]{1,0:T(4,128)} %bitcast.9, s32[1,4]{1,0:T(1,128)} %count_hbm.1, bf16[512,512]{1,0:T(8,128)(2,1)} %amps_hbm.1, f32[1,512]{1,0:T(1,128)} %bitcast.10, f32[1,512]{1,0:T(1,128)} %bitcast.11, bf16[64,128,128]{2,1,0:T(8,128)(2,1)} %bitcast.7, ...), custom_call_target="tpu_custom_call" | custom-call | flops 4000000000 | bytes 5000000 | tf_op jit(solution)/shard_map/pallas_call | solution.py:426
  86.3 2.3 %copy.11 = f32[512,512]{1,0:T(8,128)} copy(f32[512,512]{1,0:T(8,128)} %shard_map.91) | data formatting | bytes 2097152

commit v3 on v2

--- a/solution.py
+++ b/solution.py
@@ -14,6 +14,7 @@
 SLOTS = 16
 CODES = 1024
 KP = 4
+WIDE = 4
 MESH = pl.DeviceIdType.MESH
 
 FIRST = 7
@@ -32,7 +33,7 @@
     virt_energy_hbm,
     ladder_hbm,
     cycle_hbm,
-    out_hbm,
+    out_ref,
     owner_ref,
     slot_ref,
     lists_ref,
@@ -44,7 +45,6 @@
     amps_ref,
     pair_energy_ref,
     virt_energy_ref,
-    out_ref,
     ladder_ref,
     cycle_ref,
     held,
@@ -67,6 +67,7 @@
     slot_recv,
     back_send,
     back_recv,
+    meet,
 ):
     p = lax.axis_index("pair")
     q = lax.axis_index("panel")
@@ -97,19 +98,24 @@
     for load in loads:
         load.start()
 
+    row = 2 * WIDE
+    rows_in_plane = n_pair // row
+    core, x, y = lax.rem(p, 2), lax.rem(p // 2, WIDE), p // row
+
+    def device(y, x, core):
+        y = lax.rem(y + rows_in_plane, rows_in_plane)
+        return ((y * WIDE + lax.rem(x + WIDE, WIDE)) * 2 + core, q)
+
+    across = [device(y, x, 1 - core)]
+    along_x = [device(y, x + 1, core), device(y, x - 1, core)]
+    along_y = [device(y + 1, x, core), device(y - 1, x, core)]
+
     barrier = pltpu.get_barrier_semaphore()
-    for neighbour in (left, right):
+    near = [left, right] + across + along_x + along_y
+    for neighbour in near:
         pl.semaphore_signal(barrier, inc=1, device_id=neighbour, device_id_type=MESH)
-
-    def greet(d, carry):
-        pl.semaphore_signal(
-            barrier, inc=1, device_id=(lax.rem(p + d, n_pair), q), device_id_type=MESH
-        )
-        return carry
-
-    lax.fori_loop(1, n_pair, greet, 0)
     loads[0].wait()
-    pl.semaphore_wait(barrier, n_pair + 1)
+    pl.semaphore_wait(barrier, len(near))
 
     def to_right(source, tile, s):
         return pltpu.make_async_remote_copy(
@@ -136,6 +142,13 @@
         to_right(amps_ref.at[:, pl.ds(j * TB, TB)], q * KP + j, s).start()
         to_left(amps_ref.at[:, pl.ds(k * TB, TB)], q * KP + k, s).start()
 
+    def tell(n, group):
+        for neighbour in group:
+            pl.semaphore_signal(
+                meet.at[n], inc=1, device_id=neighbour, device_id_type=MESH
+            )
+
+    tell(0, across)
     for load in loads[1:5]:
         load.wait()
     tiles = row_tiles * KP
@@ -147,13 +160,13 @@
         high = jnp.where(lane == owner_ref[0, t], t * SLOTS + slot_ref[0, t], high)
         low = jnp.where(lane == owner_ref[0, u], u * SLOTS + slot_ref[0, u], low)
     code_row[...] = low * CODES + high
-    row = lax.broadcasted_iota(jnp.int32, (KP, TB), 0)
+    output = lax.broadcasted_iota(jnp.int32, (KP, TB), 0)
     column = lax.broadcasted_iota(jnp.int32, (KP, TB), 1)
     inv = jnp.zeros((KP, TB), jnp.int32)
     for k in range(KP):
         for i in range(LMAX):
             named = jnp.where(i < count_ref[0, k], lists_ref[k, i], -1)
-            inv = jnp.where((row == k) & (column == named), i + 1, inv)
+            inv = jnp.where((output == k) & (column == named), i + 1, inv)
     inv_rows[...] = inv
     tables = [
         pltpu.make_async_copy(code_row, code_ref, local_sem.at[9]),
@@ -161,6 +174,8 @@
     ]
     for table in tables:
         table.start()
+    pl.semaphore_wait(meet.at[0], 1)
+    tell(1, along_x)
 
     for r in range(row_tiles):
         for k in range(KP):
@@ -176,8 +191,16 @@
         for c, code in enumerate(codes_of(code_ref[0, peer])):
             target[place, c] = own[lax.shift_right_logical(code, 4)]
 
-    def dispatch(d, carry):
-        peer = lax.rem(p + d, n_pair)
+    def steps_of(i):
+        h = (i // row + 1) // 2
+        return lax.select(lax.rem(i // row, 2) == 1, h, rows_in_plane - h), lax.rem(i, row)
+
+    def at(down, over):
+        return lax.rem(y + down, rows_in_plane) * row + lax.rem(p + over, row)
+
+    def dispatch(i, carry):
+        down, over = steps_of(i)
+        peer = at(down, over)
         fill(peer, send, peer)
         pltpu.make_async_remote_copy(
             src_ref=send.at[peer],
@@ -197,7 +220,13 @@
         ).start()
         return carry
 
-    lax.fori_loop(1, n_pair, dispatch, 0)
+    pl.semaphore_wait(meet.at[1], 2)
+    lax.fori_loop(1, row, dispatch, 0)
+    for r in range(1, rows_in_plane // 2 + 1):
+        tell(1 + r, along_y)
+        pl.semaphore_wait(meet.at[1 + r], 2)
+        begin = (2 * r - 1) * row
+        lax.fori_loop(begin, min(begin + 2 * row, n_pair), dispatch, 0)
     fill(p, got, p)
     got_slot[p] = code_row[...]
 
@@ -282,7 +311,10 @@
             ).astype(jnp.bfloat16)
 
     def answer(base, count):
-        sources = [lax.rem(p + n_pair - (base + u), n_pair) for u in range(count)]
+        sources = []
+        for u in range(count):
+            down, over = steps_of(base + u)
+            sources.append(at(rows_in_plane - down, row - over))
         for source in sources:
             pltpu.make_async_remote_copy(
                 src_ref=send.at[source],
@@ -391,17 +423,10 @@
     def _():
         to_left(held.at[from_left], from_left, steps).wait_recv()
 
-    stores = []
     for b in range(slab // TB):
         rows = pl.ds(b * TB, TB)
         lhs = jnp.concatenate([held[from_left, rows], held[from_right, rows]], axis=1)
         out_ref[rows] += jnp.dot(lhs, mats[...], preferred_element_type=jnp.float32)
-        stores.append(
-            pltpu.make_async_copy(out_ref.at[rows], out_hbm.at[rows], local_sem.at[b])
-        )
-        stores[-1].start()
-    for store in stores:
-        store.wait()
 
 
 def on_device(
@@ -425,9 +450,9 @@
     dma = pltpu.SemaphoreType.DMA
     return pl.pallas_call(
         functools.partial(kernel, n_pair, n_panel),
-        out_shape=jax.ShapeDtypeStruct((slab, KP * TB), jnp.float32),
+        out_shape=pltpu.VMEM((slab, KP * TB), jnp.float32),
         in_specs=[anyspace] * 9,
-        out_specs=anyspace,
+        out_specs=pl.BlockSpec(memory_space=pltpu.VMEM),
         scratch_shapes=[
             pltpu.SMEM((1, tiles), jnp.int32),
             pltpu.SMEM((1, tiles), jnp.int32),
@@ -440,7 +465,6 @@
             pltpu.VMEM((slab, KP * TB), jnp.bfloat16),
             pltpu.VMEM((1, slab), jnp.float32),
             pltpu.VMEM((1, KP * TB), jnp.float32),
-            pltpu.VMEM((slab, KP * TB), jnp.float32),
             pltpu.VMEM((KP * LMAX, TB, TB), jnp.bfloat16),
             pltpu.VMEM((cycle_tiles.shape[1], TB, TB), jnp.bfloat16),
             pltpu.VMEM((n_panel * KP, slab, TB), jnp.bfloat16),
@@ -463,6 +487,7 @@
             dma(()),
             dma(()),
             dma(()),
+            pltpu.SemaphoreType.REGULAR((2 + n_pair // (4 * WIDE),)),
         ],
         compiler_params=pltpu.CompilerParams(
             collective_id=0, has_side_effects=True, vmem_limit_bytes=60 * 1024 * 1024

time: 88.7 us -> 83.1 us (0.937); the launches traced: 88.6 us -> 81.8 us
  Pallas kernels: 86.3 us -> 80.8 us
  local copies, waits for them, and re-layouts: 2.26 us -> 0.97 us
    pallas_call x1, Pallas kernels: 86.3 us -> 80.8 us  [on_device(): pl.pallas_call(functools.partial(kernel, n_pair, n_panel), out_shape=pltp...]
    unnamed x1, local copies, waits for them, and re-layouts: 2.26 us -> 0.97 us
where the time goes in v3:
time: 83.1 us; the launch traced here: 81.8 us
  Pallas kernels  80.8 us (97%)
  local copies, waits for them, and re-layouts  0.97 us (1%)
    pallas_call x1, Pallas kernels, on_device(): pl.pallas_call(functools.partial(kernel, n_pair, n_panel), out_shape=pltp...  80.8 us

profile of v3, /device:TPU:1, one launch (start us, length us, event | category | flops | bytes accessed | tf_op | source)
XLA Modules:
  0.0 81.8 jit_solution(8606442900848176939)
XLA Ops:
  0.0 80.8 %shard_map.91 = f32[512,512]{1,0:T(8,128)S(1)} custom-call(s32[1,64]{1,0:T(1,128)} %bitcast.12, s32[1,64]{1,0:T(1,128)} %bitcast.13, s32[4,16]{1,0:T(4,128)} %bitcast.9, s32[1,4]{1,0:T(1,128)} %count_hbm.1, bf16[512,512]{1,0:T(8,128)(2,1)} %amps_hbm.1, f32[1,512]{1,0:T(1,128)} %bitcast.10, f32[1,512]{1,0:T(1,128)} %bitcast.11, ...), custom_call_target="tpu_custom_call" | custom-call | flops 4000000000 | bytes 5000000 | tf_op jit(solution)/shard_map/pallas_call | solution.py:451
  80.8 1.0 %copy.11 = f32[512,512]{1,0:T(8,128)} copy(f32[512,512]{1,0:T(8,128)S(1)} %shard_map.91) | data formatting | bytes 2097152

commit v4 on v3

--- a/solution.py
+++ b/solution.py
@@ -17,8 +17,8 @@
 WIDE = 4
 MESH = pl.DeviceIdType.MESH
 
-FIRST = 7
-GROUP = 9
+FIRST = 8
+GROUP = 11
 
 
 def kernel(
@@ -109,6 +109,7 @@
     across = [device(y, x, 1 - core)]
     along_x = [device(y, x + 1, core), device(y, x - 1, core)]
     along_y = [device(y + 1, x, core), device(y - 1, x, core)]
+    further_y = [device(y + 2, x, core), device(y - 2, x, core)]
 
     barrier = pltpu.get_barrier_semaphore()
     near = [left, right] + across + along_x + along_y
@@ -141,6 +142,30 @@
         j, k = s, (s + KP // 2) % KP
         to_right(amps_ref.at[:, pl.ds(j * TB, TB)], q * KP + j, s).start()
         to_left(amps_ref.at[:, pl.ds(k * TB, TB)], q * KP + k, s).start()
+
+    def arrivals(s):
+        hop = s // KP + 1
+        from_left = lax.rem(q + n_panel - hop, n_panel) * KP + lax.rem(s, KP)
+        from_right = lax.rem(q + hop, n_panel) * KP + lax.rem(s + KP // 2, KP)
+        return from_left, from_right
+
+    def forward(s):
+        from_left, from_right = arrivals(s)
+        to_right(held.at[from_left], from_left, s).wait_recv()
+
+        @pl.when((s < steps - KP) & ((s < last - KP) | (q != n_panel - 1)))
+        def _():
+            to_right(held.at[from_left], from_left, s + KP).start()
+
+        to_left(held.at[from_right], from_right, s).wait_recv()
+
+        @pl.when(s < steps - KP)
+        def _():
+            to_left(held.at[from_right], from_right, s + KP).start()
+
+        @pl.when((s == steps - KP + 1) & (q == 1))
+        def _():
+            to_left(held.at[from_right], from_right, steps).start()
 
     def tell(n, group):
         for neighbour in group:
@@ -160,20 +185,8 @@
         high = jnp.where(lane == owner_ref[0, t], t * SLOTS + slot_ref[0, t], high)
         low = jnp.where(lane == owner_ref[0, u], u * SLOTS + slot_ref[0, u], low)
     code_row[...] = low * CODES + high
-    output = lax.broadcasted_iota(jnp.int32, (KP, TB), 0)
-    column = lax.broadcasted_iota(jnp.int32, (KP, TB), 1)
-    inv = jnp.zeros((KP, TB), jnp.int32)
-    for k in range(KP):
-        for i in range(LMAX):
-            named = jnp.where(i < count_ref[0, k], lists_ref[k, i], -1)
-            inv = jnp.where((output == k) & (column == named), i + 1, inv)
-    inv_rows[...] = inv
-    tables = [
-        pltpu.make_async_copy(code_row, code_ref, local_sem.at[9]),
-        pltpu.make_async_copy(inv_rows, inv_ref, local_sem.at[10]),
-    ]
-    for table in tables:
-        table.start()
+    code_table = pltpu.make_async_copy(code_row, code_ref, local_sem.at[9])
+    code_table.start()
     pl.semaphore_wait(meet.at[0], 1)
     tell(1, along_x)
 
@@ -181,8 +194,9 @@
         for k in range(KP):
             own[r * KP + k] = amps_ref[pl.ds(r * RR, RR), pl.ds(k * TB, TB)]
 
-    for table in tables:
-        table.wait()
+    pl.semaphore_wait(meet.at[1], 2)
+    tell(2, along_y)
+    code_table.wait()
 
     def codes_of(code):
         return lax.shift_right_logical(code, 10), lax.bitwise_and(code, CODES - 1)
@@ -220,18 +234,33 @@
         ).start()
         return carry
 
-    pl.semaphore_wait(meet.at[1], 2)
     lax.fori_loop(1, row, dispatch, 0)
-    for r in range(1, rows_in_plane // 2 + 1):
-        tell(1 + r, along_y)
-        pl.semaphore_wait(meet.at[1 + r], 2)
-        begin = (2 * r - 1) * row
-        lax.fori_loop(begin, min(begin + 2 * row, n_pair), dispatch, 0)
+    rounds = [along_y] if rows_in_plane == 2 else [along_y, further_y, along_y]
+    known = [0, 1] if rows_in_plane == 2 else [0, 1, 3, 4]
+    for r in range(len(rounds)):
+        pl.semaphore_wait(meet.at[2 + r], 2)
+        if r + 1 < len(rounds):
+            tell(3 + r, rounds[r + 1])
+        begin = (2 * known[r] + 1) * row
+        end = min((2 * known[r + 1] + 1) * row, n_pair)
+        lax.fori_loop(begin, end, dispatch, 0)
+
+    output = lax.broadcasted_iota(jnp.int32, (KP, TB), 0)
+    column = lax.broadcasted_iota(jnp.int32, (KP, TB), 1)
+    inv = jnp.zeros((KP, TB), jnp.int32)
+    for k in range(KP):
+        for i in range(LMAX):
+            named = jnp.where(i < count_ref[0, k], lists_ref[k, i], -1)
+            inv = jnp.where((output == k) & (column == named), i + 1, inv)
+    inv_rows[...] = inv
+    inv_table = pltpu.make_async_copy(inv_rows, inv_ref, local_sem.at[10])
+    inv_table.start()
     fill(p, got, p)
     got_slot[p] = code_row[...]
 
     for load in loads[5:]:
         load.wait()
+    inv_table.wait()
     for b in range(slab // TB):
         rows = pl.ds(b * TB, TB)
         column = jnp.transpose(
@@ -266,32 +295,11 @@
             amps_ref[:, pl.ds(j * TB, TB)], amps_ref[:, pl.ds((j + 1) * TB, TB)]
         )
 
-    def arrivals(s):
-        hop = s // KP + 1
-        from_left = lax.rem(q + n_panel - hop, n_panel) * KP + lax.rem(s, KP)
-        from_right = lax.rem(q + hop, n_panel) * KP + lax.rem(s + KP // 2, KP)
-        return from_left, from_right
-
-    def ring(s):
+    def accumulate(s, carry):
         from_left, from_right = arrivals(s)
-        to_right(held.at[from_left], from_left, s).wait_recv()
-
-        @pl.when((s < steps - KP) & ((s < last - KP) | (q != n_panel - 1)))
-        def _():
-            to_right(held.at[from_left], from_left, s + KP).start()
-
-        to_left(held.at[from_right], from_right, s).wait_recv()
-
-        @pl.when(s < steps - KP)
-        def _():
-            to_left(held.at[from_right], from_right, s + KP).start()
-
-        @pl.when((s == steps - KP + 1) & (q == 1))
-        def _():
-            to_left(held.at[from_right], from_right, steps).start()
-
         pick(from_left, from_right)
         add_ladder(held[from_left], held[from_right])
+        return carry
 
     def back(source, s):
         return pltpu.make_async_remote_copy(
@@ -336,11 +344,12 @@
     first = min(FIRST, max(0, last - chunks))
 
     def plain(s, carry):
-        ring(s)
-        return carry
+        forward(s)
+        return accumulate(s, carry)
 
     def both(s, carry):
-        ring(s)
+        forward(s)
+        accumulate(s, carry)
         answer(1 + (s - first) * group, group)
         return carry
 
@@ -487,7 +496,7 @@
             dma(()),
             dma(()),
             dma(()),
-            pltpu.SemaphoreType.REGULAR((2 + n_pair // (4 * WIDE),)),
+            pltpu.SemaphoreType.REGULAR((2 + 3,)),
         ],
         compiler_params=pltpu.CompilerParams(
             collective_id=0, has_side_effects=True, vmem_limit_bytes=60 * 1024 * 1024

time: 83.1 us -> 80.4 us (0.968); the launches traced: 81.8 us -> 80 us
  Pallas kernels: 80.8 us -> 79 us
    pallas_call x1, Pallas kernels: 80.8 us -> 79 us  [on_device(): pl.pallas_call(functools.partial(kernel, n_pair, n_panel), out_shape=pltp...]
where the time goes in v4:
time: 80.4 us; the launch traced here: 80 us
  Pallas kernels  79 us (98%)
  local copies, waits for them, and re-layouts  0.97 us (1%)
    pallas_call x1, Pallas kernels, on_device(): pl.pallas_call(functools.partial(kernel, n_pair, n_panel), out_shape=pltp...  79 us

profile of v4, /device:TPU:1, one launch (start us, length us, event | category | flops | bytes accessed | tf_op | source)
XLA Modules:
  0.0 80.0 jit_solution(7747959769746128944)
XLA Ops:
  0.0 79.0 %shard_map.91 = f32[512,512]{1,0:T(8,128)S(1)} custom-call(s32[1,64]{1,0:T(1,128)} %bitcast.12, s32[1,64]{1,0:T(1,128)} %bitcast.13, s32[4,16]{1,0:T(4,128)} %bitcast.9, s32[1,4]{1,0:T(1,128)} %count_hbm.1, bf16[512,512]{1,0:T(8,128)(2,1)} %amps_hbm.1, f32[1,512]{1,0:T(1,128)} %bitcast.10, f32[1,512]{1,0:T(1,128)} %bitcast.11, ...), custom_call_target="tpu_custom_call" | custom-call | flops 4000000000 | bytes 5000000 | tf_op jit(solution)/shard_map/pallas_call | solution.py:460
  79.0 1.0 %copy.11 = f32[512,512]{1,0:T(8,128)} copy(f32[512,512]{1,0:T(8,128)S(1)} %shard_map.91) | data formatting | bytes 2097152
